TPU v7x, 32 devices: a whole 2x2x4 slice. The times are simulated.
32 devices in a mesh: grid: 16 (over z, y, x), mode: 2 (over core).
Axes of the slice: x: 2, y: 2, z: 4, core: 2. Of those that a mesh axis runs over, the one named last changes fastest.
Arguments:
- modes: bfloat16 [8, 3, 32, 32, 128], P('mode', None, 'grid'), may hold values from -0.29882812 to 0.29882812
- eigenvalues: float32 [8], P('mode'), may hold values from 2 to 50
- density: float32 [32, 32, 128], P('grid'), may hold values from 0.1 to 1
Outputs:
- gradient: float32 [32, 32, 128], P('grid')
All inputs are finite; a program needn't handle non-finite values.
Results may differ from a plain program's by a relative error of at most 0.006.
Values may be sent and summed in bfloat16 or wider, within the bound.
A program may use at most 64 MiB of HBM per device.

v0:
```python
import jax
import jax.numpy as jnp
import numpy as np
from jax import lax
from jax.sharding import PartitionSpec as P


def shifted(value, axis, steps):
    count = lax.axis_size(axis)
    first, last = (max(0, -steps), min(count, count - steps))
    return lax.ppermute(value, axis, [(source, source + steps) for source in range(first, last)])


def padded_2(block, sides, width):
    for axis, dim in sides:
        count = lax.axis_size(axis)
        forward = [(i, i + 1) for i in range(count - 1)]
        backward = [(target, source) for source, target in forward]
        low = lax.ppermute(
            lax.slice_in_dim(block, block.shape[dim] - width, None, axis=dim), axis, forward
        )
        high = lax.ppermute(lax.slice_in_dim(block, 0, width, axis=dim), axis, backward)
        block = jnp.concatenate([low, block, high], axis=dim)
    return block


def element_tables():
    poisson = 0.3
    lame_first = poisson / ((1.0 + poisson) * (1.0 - 2.0 * poisson))
    shear = 0.5 / (1.0 + poisson)
    elastic = np.zeros((6, 6))
    elastic[:3, :3] = lame_first
    for axis_bit in range(3):
        elastic[axis_bit, axis_bit] += 2.0 * shear
        elastic[axis_bit + 3, axis_bit + 3] = shear
    stiffness = np.zeros((24, 24))
    mass_small = np.zeros((8, 8))
    point = 1.0 / np.sqrt(3.0)
    for gauss in range(8):
        coords = [point * (2 * (gauss >> axis_bit & 1) - 1) for axis_bit in range(3)]
        shape_values = np.zeros(8)
        grads = np.zeros((3, 8))
        for corner in range(8):
            signs = [2 * (corner >> axis_bit & 1) - 1 for axis_bit in range(3)]
            factors = [1.0 + signs[axis_bit] * coords[axis_bit] for axis_bit in range(3)]
            shape_values[corner] = 0.125 * factors[0] * factors[1] * factors[2]
            grads[0, corner] = 0.25 * signs[0] * factors[1] * factors[2]
            grads[1, corner] = 0.25 * signs[1] * factors[0] * factors[2]
            grads[2, corner] = 0.25 * signs[2] * factors[0] * factors[1]
        strain = np.zeros((6, 24))
        for corner in range(8):
            column = 3 * corner
            strain[0, column] = grads[0, corner]
            strain[1, column + 1] = grads[1, corner]
            strain[2, column + 2] = grads[2, corner]
            strain[3, column] = grads[1, corner]
            strain[3, column + 1] = grads[0, corner]
            strain[4, column + 1] = grads[2, corner]
            strain[4, column + 2] = grads[1, corner]
            strain[5, column] = grads[2, corner]
            strain[5, column + 2] = grads[0, corner]
        stiffness = stiffness + strain.T @ elastic @ strain * 0.125
        mass_small = mass_small + np.outer(shape_values, shape_values) * 0.125
    mass = np.kron(mass_small, np.eye(3))
    return np.concatenate([stiffness, mass], 0).astype(np.float32)


def element_forms(field, table):
    depth = field.shape[1] - 1
    height = field.shape[2]
    width = field.shape[3]
    padded = jnp.pad(field, ((0, 0), (0, 0), (0, 1), (0, 1)))
    pieces = []
    for corner in range(8):
        x_off = corner & 1
        y_off = corner >> 1 & 1
        z_off = corner >> 2
        for component in range(3):
            pieces.append(
                padded[
                    component, z_off : z_off + depth, y_off : y_off + height, x_off : x_off + width
                ].reshape(-1)
            )
    stacked = jnp.stack(pieces)
    images = jnp.dot(table, stacked, preferred_element_type=jnp.float32)
    values = stacked.astype(jnp.float32)
    stiff_form = jnp.sum(values * images[:24], 0).reshape(depth, height, width)
    mass_form = jnp.sum(values * images[24:], 0).reshape(depth, height, width)
    return (stiff_form, mass_form)


def stencil_bands(width):
    offsets = []
    bands = []
    for z_step in range(-2, 3):
        for y_step in range(-2, 3):
            band = np.zeros((width, width), np.float32)
            used = False
            for x_step in range(-2, 3):
                weight = 2.5 - float(np.sqrt(z_step * z_step + y_step * y_step + x_step * x_step))
                if weight > 0.0:
                    band = band + weight * np.eye(width, k=-x_step, dtype=np.float32)
                    used = True
            if used:
                offsets.append((z_step, y_step))
                bands.append(band)
    return (offsets, np.stack(bands))


def apply_stencil(padded, width):
    depth = padded.shape[0] - 4
    height = padded.shape[1] - 4
    offsets, bands = stencil_bands(width)
    stacked = jnp.stack(
        [
            padded[2 + z_step : 2 + z_step + depth, 2 + y_step : 2 + y_step + height, :]
            for z_step, y_step in offsets
        ]
    )
    return jnp.einsum(
        "kzyx,kxw->zyw",
        stacked,
        jnp.asarray(bands),
        precision=lax.Precision.HIGHEST,
        preferred_element_type=jnp.float32,
    )


def local(modes, eigenvalues, density):
    table = jnp.asarray(element_tables()).astype(jnp.bfloat16)
    count = modes.shape[0]
    stiff_total = jnp.zeros(density.shape, jnp.float32)
    mass_total = jnp.zeros(density.shape, jnp.float32)
    upper = shifted(modes[:, :, :1], "grid", -1)
    for index in range(count):
        field = jnp.concatenate([modes[index], upper[index]], 1)
        stiff_form, mass_form = element_forms(field, table)
        stiff_total = stiff_total + stiff_form
        mass_total = mass_total + eigenvalues[index] * mass_form
    slope = 3.0 * (1.0 - 0.001) * density * density
    sensitivity = slope * stiff_total - mass_total
    depth = density.shape[0]
    height = density.shape[1]
    width = density.shape[2]
    layers = lax.axis_index("grid") * depth + jnp.arange(-2, depth + 2, dtype=jnp.int32)
    inside = ((layers >= 0) & (layers < depth * lax.axis_size("grid"))).astype(jnp.float32)
    covered = jnp.broadcast_to(inside[:, None, None], (depth + 4, height, width))
    covered = jnp.pad(covered, ((0, 0), (2, 2), (0, 0)))
    totals = apply_stencil(covered, width)
    scaled = sensitivity / totals
    scaled = lax.psum(scaled.astype(jnp.bfloat16), "mode").astype(jnp.float32)
    widened = padded_2(scaled.astype(jnp.bfloat16), (("grid", 0),), 2).astype(scaled.dtype)
    widened = jnp.pad(widened, ((0, 0), (2, 2), (0, 0)))
    result = apply_stencil(widened, width)
    return result


def solution(mesh):
    in_specs = (P("mode", None, "grid", None, None), P("mode"), P("grid", None, None))
    out_specs = P("grid", None, None)
    return jax.shard_map(local, mesh=mesh, in_specs=in_specs, out_specs=out_specs, check_vma=False)
```

profile of v0, /device:TPU:6, one launch (start us, length us, event | category | flops | bytes accessed | tf_op | source)
XLA Modules:
  0.0 120.0 jit_solution(660327422919352532)
XLA Ops:
  0.0 0.9 slice_bitcast_fusion
  0.9 2.4 %collective-permute-start = (bf16[4,3,1,32,128]{4,3,1,2,0:T(8,128)(2,1)S(1)}, bf16[4,3,1,32,128]{4,3,1,2,0:T(8,128)(2,1)S(1)}, u32[]{:S(2)}, u32[]{:S(2)}) collective-permute-start(bf16[4,3,1,32,128]{4,3,1,2,0:T(8,128)(2,1)S(1)} %slice_bitcast_fusion), channel_id=1, source_target_pairs={{2,0},{4,2},{6,4},{8,6},{10,8},{12,10},{14,12},{16,14},{18,16},{20... | collective-permute-start | bytes 294920 | tf_op jit(solution)/shard_map/ppermute | solution.py:11
  3.3 0.9 slice_bitcast_fusion.4
  4.2 0.9 fusion.56
  5.9 0.6 copy.266
  6.6 0.6 copy.244
  8.0 0.8 copy_bitcast_fusion.69
  8.7 0.7 copy_bitcast_fusion.45
  9.4 0.7 copy_bitcast_fusion.21
  10.1 0.7 fusion.57
  11.9 0.6 copy.299
  16.7 0.6 copy.272
  18.0 0.6 copy.274
  19.9 0.6 copy.280
  21.1 0.6 copy.282
  22.4 0.6 copy.284
  24.9 0.6 copy.276
  26.1 0.6 copy.278
  29.0 0.6 copy.246
  32.7 0.6 copy.252
  34.6 0.6 copy.258
  37.1 0.6 copy.262
  38.4 0.6 copy.264
  40.9 0.6 copy.256
  55.0 0.6 copy.224
  57.5 0.6 copy.228
  59.4 0.6 copy.231
  61.9 0.6 copy.238
  63.2 0.6 copy.240
  65.7 0.6 copy.232
  66.9 0.6 copy.234
  67.6 1.9 %stack.144 = bf16[24,8192]{1,0:T(8,128)(2,1)S(1)} concatenate(bf16[1,8192]{1,0:T(2,128)(2,1)S(1)} %bitcast.1095, bf16[1,8192]{1,0:T(2,128)(2,1)S(1)} %get-tuple-element.143, bf16[1,8192]{1,0:T(2,128)(2,1)S(1)} %get-tuple-element.142, bf16[1,8192]{1,0:T(2,128)(2,1)S(1)} %bitcast.1125, bf16[1,8192]{1,0:T(2,128)(2,1)S(1)} %bitcast.1123, bf16[1,8192]{1,0:T(2,128)(2,1)S(1)} %bitcast.1121, ...), dimensions={0} | concatenate | bytes 786432 | tf_op jit(solution)/shard_map/stack | solution.py:84
  69.5 3.8 %multiply_add_fusion.69 = f32[48,8192]{1,0:T(8,128)S(1)} fusion(f32[8192]{0:T(1024)S(1)} %convert.311, f32[48]{0:T(128)} %constant.114, f32[8192]{0:T(1024)S(1)} %convert.310, f32[48]{0:T(128)S(1)} %copy-done.36, f32[8192]{0:T(1024)S(1)} %convert.309, f32[48]{0:T(128)S(1)} %copy-done.35, f32[8192]{0:T(1024)S(1)} %convert.308, f32[48]{0:T(128)S(1)} %copy-done.34, ...), kind=kLoop, calls=%fused_computation.69 | loop fusion | flops 18481152 | bytes 2363904 | tf_op jit(solution)/shard_map/dot_general | solution.py:85
  73.5 0.9 fusion.2
  74.6 3.1 %multiply_add_fusion.46 = f32[48,8192]{1,0:T(8,128)S(1)} fusion(f32[8192]{0:T(1024)S(1)} %convert.335, f32[8192]{0:T(1024)S(1)} %convert.334, f32[8192]{0:T(1024)S(1)} %convert.333, f32[8192]{0:T(1024)S(1)} %convert.332, f32[8192]{0:T(1024)S(1)} %convert.331, f32[8192]{0:T(1024)S(1)} %convert.330, f32[8192]{0:T(1024)S(1)} %convert.329, ...), kind=kLoop, calls=%fused_computation.46 | loop fusion | flops 18481152 | bytes 2363904 | tf_op jit(solution)/shard_map/dot_general | solution.py:85
  77.9 3.8 %stack.145 = bf16[24,8192]{1,0:T(8,128)(2,1)S(1)} concatenate(bf16[1,8192]{1,0:T(2,128)(2,1)} %bitcast.1094, bf16[1,8192]{1,0:T(2,128)(2,1)} %get-tuple-element.141, bf16[1,8192]{1,0:T(2,128)(2,1)S(1)} %get-tuple-element.140, bf16[1,8192]{1,0:T(2,128)(2,1)} %bitcast.1134, bf16[1,8192]{1,0:T(2,128)(2,1)} %bitcast.1133, bf16[1,8192]{1,0:T(2,128)(2,1)} %bitcast.1132, ...), dimensions={0} | concatenate | bytes 786432 | tf_op jit(solution)/shard_map/stack | solution.py:84
  81.7 0.8 fusion.4
  82.8 2.9 %multiply_add_fusion.23 = f32[48,8192]{1,0:T(8,128)S(1)} fusion(f32[8192]{0:T(1024)S(1)} %convert.359, f32[8192]{0:T(1024)S(1)} %convert.358, f32[8192]{0:T(1024)S(1)} %convert.357, f32[8192]{0:T(1024)S(1)} %convert.356, f32[8192]{0:T(1024)S(1)} %convert.355, f32[8192]{0:T(1024)S(1)} %convert.354, f32[8192]{0:T(1024)S(1)} %convert.353, ...), kind=kLoop, calls=%fused_computation.23 | loop fusion | flops 18481152 | bytes 2363904 | tf_op jit(solution)/shard_map/dot_general | solution.py:85
  86.1 3.7 %stack.146 = bf16[24,8192]{1,0:T(8,128)(2,1)S(1)} concatenate(bf16[1,8192]{1,0:T(2,128)(2,1)S(1)} %bitcast.1093, bf16[1,8192]{1,0:T(2,128)(2,1)S(1)} %copy-done.30, bf16[1,8192]{1,0:T(2,128)(2,1)S(1)} %copy-done.29, bf16[1,8192]{1,0:T(2,128)(2,1)} %bitcast.1166, bf16[1,8192]{1,0:T(2,128)(2,1)} %bitcast.1164, bf16[1,8192]{1,0:T(2,128)(2,1)} %bitcast.1162, ...), dimensions={0} | concatenate | bytes 786432 | tf_op jit(solution)/shard_map/stack | solution.py:84
  90.4 3.6 %multiply_add_fusion = f32[48,8192]{1,0:T(8,128)S(1)} fusion(f32[8192]{0:T(1024)S(1)} %copy-done.23, f32[8192]{0:T(1024)S(1)} %copy-done.22, f32[8192]{0:T(1024)S(1)} %copy-done.21, f32[8192]{0:T(1024)S(1)} %copy-done.20, f32[8192]{0:T(1024)S(1)} %copy-done.19, f32[8192]{0:T(1024)S(1)} %copy-done.18, f32[8192]{0:T(1024)S(1)} %copy-done.17, ...), kind=kLoop, calls=%fused_computation | loop fusion | flops 18481152 | bytes 2363904 | tf_op jit(solution)/shard_map/dot_general | solution.py:85
  94.1 3.8 %stack.147 = bf16[24,8192]{1,0:T(8,128)(2,1)S(1)} concatenate(bf16[1,8192]{1,0:T(2,128)(2,1)} %bitcast.1092, bf16[1,8192]{1,0:T(2,128)(2,1)} %get-tuple-element.137, bf16[1,8192]{1,0:T(2,128)(2,1)} %get-tuple-element.136, bf16[1,8192]{1,0:T(2,128)(2,1)} %bitcast.1176, bf16[1,8192]{1,0:T(2,128)(2,1)} %bitcast.1175, bf16[1,8192]{1,0:T(2,128)(2,1)} %bitcast.1174, ...), dimensions={0} | concatenate | bytes 786432 | tf_op jit(solution)/shard_map/stack | solution.py:84
  98.2 2.7 %multiply_add_fusion.92 = f32[8192]{0:T(1024)S(1)} fusion(f32[8192]{0:T(1024)S(1)} %get-tuple-element.12, f32[8192]{0:T(1024)S(1)} %get-tuple-element.10, f32[8192]{0:T(1024)S(1)} %copy-done.28, f32[8192]{0:T(1024)S(1)} %copy-done.27, f32[]{:T(128)} %bitcast.111, f32[]{:T(128)} %bitcast.110, f32[]{:T(128)} %bitcast.109, f32[]{:T(128)} %bitcast.108), kind=kLoop, calls=%fused_computation.428 | loop fusion | flops 57344 | bytes 163856 | tf_op jit(solution)/shard_map/add | solution.py:139
  101.0 1.0 fusion.1
  102.0 3.5 %psum.7 = bf16[2,32,128]{2,1,0:T(8,128)(2,1)S(1)} all-reduce(bf16[2,32,128]{2,1,0:T(8,128)(2,1)S(1)} %fusion.1), channel_id=1, replica_groups=mesh['grid'=16,'mode'=2] {'mode'}, use_global_device_ids=true, to_apply=%region_8.9 | all-reduce | flops 8192 | bytes 32768 | tf_op jit(solution)/shard_map/psum | solution.py:151
  105.5 5.2 %collective-permute-start.1 = (bf16[2,32,128]{2,1,0:T(8,128)(2,1)S(1)}, bf16[2,32,128]{2,1,0:T(8,128)(2,1)S(1)}, u32[]{:S(2)}, u32[]{:S(2)}) collective-permute-start(bf16[2,32,128]{2,1,0:T(8,128)(2,1)S(1)} %psum.7), channel_id=1, source_target_pairs={{0,2},{2,4},{4,6},{6,8},{8,10},{10,12},{12,14},{14,16},{16,18},{18... | collective-permute-start | bytes 49160 | tf_op jit(solution)/shard_map/ppermute | solution.py:19
  110.7 1.9 %collective-permute-start.2 = (bf16[2,32,128]{2,1,0:T(8,128)(2,1)S(1)}, bf16[2,32,128]{2,1,0:T(8,128)(2,1)S(1)}, u32[]{:S(2)}, u32[]{:S(2)}) collective-permute-start(bf16[2,32,128]{2,1,0:T(8,128)(2,1)S(1)} %psum.7), channel_id=1, source_target_pairs={{2,0},{4,2},{6,4},{8,6},{10,8},{12,10},{14,12},{16,14},{18,16},{20... | collective-permute-start | bytes 49160 | tf_op jit(solution)/shard_map/ppermute | solution.py:22
  112.6 5.5 %collective-permute-done.2 = bf16[2,32,128]{2,1,0:T(8,128)(2,1)S(1)} collective-permute-done((bf16[2,32,128]{2,1,0:T(8,128)(2,1)S(1)}, bf16[2,32,128]{2,1,0:T(8,128)(2,1)S(1)}, u32[]{:S(2)}, u32[]{:S(2)}) %collective-permute-start.2) | collective-permute-done | bytes 16416 | tf_op jit(solution)/shard_map/ppermute | solution.py:22
  118.4 1.6 %convolution_bitcast_fusion = f32[2,32,128]{2,1,0:T(8,128)} fusion(f32[21,2,32,128]{3,2,1,0:T(8,128)S(1)} %constant_dynamic-update-slice_fusion.21, f32[21,128,128,1]{2,1,3,0:T(8,128)S(1)} %copy-done), kind=kOutput, calls=%fused_computation.92 | convolution fusion | flops 264241152 | bytes 2097152 | tf_op jit(solution)/shard_map/kzyx,kxw->zyw/dot_general | solution.py:120
  (411 shorter events, 45.3 us)
Async XLA Ops:
  0.9 9.9 %collective-permute-start = (bf16[4,3,1,32,128]{4,3,1,2,0:T(8,128)(2,1)S(1)}, bf16[4,3,1,32,128]{4,3,1,2,0:T(8,128)(2,1)S(1)}, u32[]{:S(2)}, u32[]{:S(2)}) collective-permute-start(bf16[4,3,1,32,128]{4,3,1,2,0:T(8,128)(2,1)S(1)} %slice_bitcast_fusion), channel_id=1, source_target_pairs={{2,0},{4,2},{6,4},{8,6},{10,8},{12,10},{14,12},{16,14},{18,16},{20... | collective-permute-start | bytes 294920 | tf_op jit(solution)/shard_map/ppermute | solution.py:11
  44.7 24.8 %copy-start.33 = (f32[48]{0:T(128)S(1)}, f32[48]{0:T(128)}, u32[]{:S(2)}) copy-start(f32[48]{0:T(128)} %constant.102) | copy-start | bytes 580
  44.7 24.8 %copy-start.34 = (f32[48]{0:T(128)S(1)}, f32[48]{0:T(128)}, u32[]{:S(2)}) copy-start(f32[48]{0:T(128)} %constant.105) | copy-start | bytes 580
  44.7 24.8 %copy-start.35 = (f32[48]{0:T(128)S(1)}, f32[48]{0:T(128)}, u32[]{:S(2)}) copy-start(f32[48]{0:T(128)} %constant.108) | copy-start | bytes 580
  44.7 24.8 %copy-start.36 = (f32[48]{0:T(128)S(1)}, f32[48]{0:T(128)}, u32[]{:S(2)}) copy-start(f32[48]{0:T(128)} %constant.111) | copy-start | bytes 580
  77.7 4.9 %copy-start.4 = (f32[8192]{0:T(1024)S(1)}, f32[8192]{0:T(1024)}, u32[]{:S(2)}) copy-start(f32[8192]{0:T(1024)} %convert.349) | copy-start | bytes 98308
  77.7 4.9 %copy-start.5 = (f32[8192]{0:T(1024)S(1)}, f32[8192]{0:T(1024)}, u32[]{:S(2)}) copy-start(f32[8192]{0:T(1024)} %convert.350) | copy-start | bytes 98308
  77.7 4.9 %copy-start.38 = (f32[48]{0:T(128)S(1)}, f32[48]{0:T(128)}, u32[]{:S(2)}) copy-start(f32[48]{0:T(128)} %constant.114) | copy-start | bytes 580
  77.7 4.9 %copy-start.41 = (f32[48]{0:T(128)S(1)}, f32[48]{0:T(128)}, u32[]{:S(2)}) copy-start(f32[48]{0:T(128)} %constant.45) | copy-start | bytes 580
  77.7 4.8 %copy-start.44 = (f32[48]{0:T(128)S(1)}, f32[48]{0:T(128)}, u32[]{:S(2)}) copy-start(f32[48]{0:T(128)} %constant.48) | copy-start | bytes 580
  77.7 4.8 %copy-start.47 = (f32[48]{0:T(128)S(1)}, f32[48]{0:T(128)}, u32[]{:S(2)}) copy-start(f32[48]{0:T(128)} %constant.51) | copy-start | bytes 580
  77.7 4.8 %copy-start.50 = (f32[48]{0:T(128)S(1)}, f32[48]{0:T(128)}, u32[]{:S(2)}) copy-start(f32[48]{0:T(128)} %constant.54) | copy-start | bytes 580
  77.7 4.8 %copy-start.53 = (f32[48]{0:T(128)S(1)}, f32[48]{0:T(128)}, u32[]{:S(2)}) copy-start(f32[48]{0:T(128)} %constant.57) | copy-start | bytes 580
  77.8 4.8 %copy-start.56 = (f32[48]{0:T(128)S(1)}, f32[48]{0:T(128)}, u32[]{:S(2)}) copy-start(f32[48]{0:T(128)} %constant.60) | copy-start | bytes 580
  77.8 4.8 %copy-start.59 = (f32[48]{0:T(128)S(1)}, f32[48]{0:T(128)}, u32[]{:S(2)}) copy-start(f32[48]{0:T(128)} %constant.63) | copy-start | bytes 580
  77.8 4.8 %copy-start.62 = (f32[48]{0:T(128)S(1)}, f32[48]{0:T(128)}, u32[]{:S(2)}) copy-start(f32[48]{0:T(128)} %constant.66) | copy-start | bytes 580
  77.8 4.8 %copy-start.65 = (f32[48]{0:T(128)S(1)}, f32[48]{0:T(128)}, u32[]{:S(2)}) copy-start(f32[48]{0:T(128)} %constant.69) | copy-start | bytes 580
  77.8 4.8 %copy-start.68 = (f32[48]{0:T(128)S(1)}, f32[48]{0:T(128)}, u32[]{:S(2)}) copy-start(f32[48]{0:T(128)} %constant.72) | copy-start | bytes 580
  77.8 4.8 %copy-start.71 = (f32[48]{0:T(128)S(1)}, f32[48]{0:T(128)}, u32[]{:S(2)}) copy-start(f32[48]{0:T(128)} %constant.75) | copy-start | bytes 580
  77.8 4.8 %copy-start.74 = (f32[48]{0:T(128)S(1)}, f32[48]{0:T(128)}, u32[]{:S(2)}) copy-start(f32[48]{0:T(128)} %constant.78) | copy-start | bytes 580
  77.8 4.8 %copy-start.77 = (f32[48]{0:T(128)S(1)}, f32[48]{0:T(128)}, u32[]{:S(2)}) copy-start(f32[48]{0:T(128)} %constant.81) | copy-start | bytes 580
  77.9 4.8 %copy-start.80 = (f32[48]{0:T(128)S(1)}, f32[48]{0:T(128)}, u32[]{:S(2)}) copy-start(f32[48]{0:T(128)} %constant.84) | copy-start | bytes 580
  77.9 4.8 %copy-start.83 = (f32[48]{0:T(128)S(1)}, f32[48]{0:T(128)}, u32[]{:S(2)}) copy-start(f32[48]{0:T(128)} %constant.87) | copy-start | bytes 580
  77.9 4.8 %copy-start.86 = (f32[48]{0:T(128)S(1)}, f32[48]{0:T(128)}, u32[]{:S(2)}) copy-start(f32[48]{0:T(128)} %constant.90) | copy-start | bytes 580
  77.9 4.8 %copy-start.88 = (f32[48]{0:T(128)S(1)}, f32[48]{0:T(128)}, u32[]{:S(2)}) copy-start(f32[48]{0:T(128)} %constant.93) | copy-start | bytes 580
  77.9 4.8 %copy-start.90 = (f32[48]{0:T(128)S(1)}, f32[48]{0:T(128)}, u32[]{:S(2)}) copy-start(f32[48]{0:T(128)} %constant.96) | copy-start | bytes 580
  77.9 4.8 %copy-start.92 = (f32[48]{0:T(128)S(1)}, f32[48]{0:T(128)}, u32[]{:S(2)}) copy-start(f32[48]{0:T(128)} %constant.99) | copy-start | bytes 580
  85.7 4.4 %copy-start.6 = (f32[8192]{0:T(1024)S(1)}, f32[8192]{0:T(1024)}, u32[]{:S(2)}) copy-start(f32[8192]{0:T(1024)} %convert.363) | copy-start | bytes 98308
  85.7 4.4 %copy-start.7 = (f32[8192]{0:T(1024)S(1)}, f32[8192]{0:T(1024)}, u32[]{:S(2)}) copy-start(f32[8192]{0:T(1024)} %convert.364) | copy-start | bytes 98308
  85.7 4.4 %copy-start.8 = (f32[8192]{0:T(1024)S(1)}, f32[8192]{0:T(1024)}, u32[]{:S(2)}) copy-start(f32[8192]{0:T(1024)} %convert.365) | copy-start | bytes 98308
  85.7 4.4 %copy-start.9 = (f32[8192]{0:T(1024)S(1)}, f32[8192]{0:T(1024)}, u32[]{:S(2)}) copy-start(f32[8192]{0:T(1024)} %convert.366) | copy-start | bytes 98308
  85.7 4.4 %copy-start.10 = (f32[8192]{0:T(1024)S(1)}, f32[8192]{0:T(1024)}, u32[]{:S(2)}) copy-start(f32[8192]{0:T(1024)} %convert.367) | copy-start | bytes 98308
  85.7 4.4 %copy-start.11 = (f32[8192]{0:T(1024)S(1)}, f32[8192]{0:T(1024)}, u32[]{:S(2)}) copy-start(f32[8192]{0:T(1024)} %convert.368) | copy-start | bytes 98308
  85.8 4.4 %copy-start.12 = (f32[8192]{0:T(1024)S(1)}, f32[8192]{0:T(1024)}, u32[]{:S(2)}) copy-start(f32[8192]{0:T(1024)} %convert.369) | copy-start | bytes 98308
  85.8 4.4 %copy-start.13 = (f32[8192]{0:T(1024)S(1)}, f32[8192]{0:T(1024)}, u32[]{:S(2)}) copy-start(f32[8192]{0:T(1024)} %convert.370) | copy-start | bytes 98308
  85.8 4.4 %copy-start.14 = (f32[8192]{0:T(1024)S(1)}, f32[8192]{0:T(1024)}, u32[]{:S(2)}) copy-start(f32[8192]{0:T(1024)} %convert.371) | copy-start | bytes 98308
  85.8 4.4 %copy-start.15 = (f32[8192]{0:T(1024)S(1)}, f32[8192]{0:T(1024)}, u32[]{:S(2)}) copy-start(f32[8192]{0:T(1024)} %convert.375) | copy-start | bytes 98308
  85.8 4.4 %copy-start.16 = (f32[8192]{0:T(1024)S(1)}, f32[8192]{0:T(1024)}, u32[]{:S(2)}) copy-start(f32[8192]{0:T(1024)} %convert.376) | copy-start | bytes 98308
  85.8 4.4 %copy-start.17 = (f32[8192]{0:T(1024)S(1)}, f32[8192]{0:T(1024)}, u32[]{:S(2)}) copy-start(f32[8192]{0:T(1024)} %convert.377) | copy-start | bytes 98308
  85.8 4.4 %copy-start.18 = (f32[8192]{0:T(1024)S(1)}, f32[8192]{0:T(1024)}, u32[]{:S(2)}) copy-start(f32[8192]{0:T(1024)} %convert.378) | copy-start | bytes 98308
  85.8 4.4 %copy-start.19 = (f32[8192]{0:T(1024)S(1)}, f32[8192]{0:T(1024)}, u32[]{:S(2)}) copy-start(f32[8192]{0:T(1024)} %convert.379) | copy-start | bytes 98308
  85.8 4.4 %copy-start.20 = (f32[8192]{0:T(1024)S(1)}, f32[8192]{0:T(1024)}, u32[]{:S(2)}) copy-start(f32[8192]{0:T(1024)} %convert.380) | copy-start | bytes 98308
  85.8 4.4 %copy-start.21 = (f32[8192]{0:T(1024)S(1)}, f32[8192]{0:T(1024)}, u32[]{:S(2)}) copy-start(f32[8192]{0:T(1024)} %convert.381) | copy-start | bytes 98308
  85.9 4.4 %copy-start.22 = (f32[8192]{0:T(1024)S(1)}, f32[8192]{0:T(1024)}, u32[]{:S(2)}) copy-start(f32[8192]{0:T(1024)} %convert.382) | copy-start | bytes 98308
  94.1 6.9 %copy-start.1 = (f32[21,128,128,1]{2,1,0,3:T(8,128)S(1)}, f32[21,128,128,1]{2,1,0,3:T(8,128)}, u32[]{:S(2)}) copy-start(f32[21,128,128,1]{2,1,0,3:T(8,128)} %constant.331) | copy-start | bytes 4128772
  102.0 16.4 %copy-start = (f32[21,128,128,1]{2,1,3,0:T(8,128)S(1)}, f32[21,128,128,1]{2,1,3,0:T(8,128)}, u32[]{:S(2)}) copy-start(f32[21,128,128,1]{2,1,3,0:T(8,128)} %constant.332) | copy-start | bytes 4128772
  105.5 7.1 %collective-permute-start.1 = (bf16[2,32,128]{2,1,0:T(8,128)(2,1)S(1)}, bf16[2,32,128]{2,1,0:T(8,128)(2,1)S(1)}, u32[]{:S(2)}, u32[]{:S(2)}) collective-permute-start(bf16[2,32,128]{2,1,0:T(8,128)(2,1)S(1)} %psum.7), channel_id=1, source_target_pairs={{0,2},{2,4},{4,6},{6,8},{8,10},{10,12},{12,14},{14,16},{16,18},{18... | collective-permute-start | bytes 49160 | tf_op jit(solution)/shard_map/ppermute | solution.py:19
  110.7 7.4 %collective-permute-start.2 = (bf16[2,32,128]{2,1,0:T(8,128)(2,1)S(1)}, bf16[2,32,128]{2,1,0:T(8,128)(2,1)S(1)}, u32[]{:S(2)}, u32[]{:S(2)}) collective-permute-start(bf16[2,32,128]{2,1,0:T(8,128)(2,1)S(1)} %psum.7), channel_id=1, source_target_pairs={{2,0},{4,2},{6,4},{8,6},{10,8},{12,10},{14,12},{16,14},{18,16},{20... | collective-permute-start | bytes 49160 | tf_op jit(solution)/shard_map/ppermute | solution.py:22
  (49 other events, 139.2 us)
where the time goes:
time: 121 us; the launch traced here: 120 us
  local copies, waits for them, and re-layouts  63.6 us (53%)
  other arithmetic  32.7 us (27%)
  starting transfers between devices  9.54 us (8%)
  waiting for transfers between devices  5.5 us (5%)
  blocking collectives  3.49 us (3%)
  between operations  2.58 us (2%)
  matrix products  2.56 us (2%)
    unnamed x317, local copies, waits for them, and re-layouts  45.2 us
    another operation x8, local copies, waits for them, and re-layouts, element_forms(): stacked = jnp.stack(pieces)  15.3 us
    unnamed x96, other arithmetic  14.3 us
    dot_general x4, other arithmetic, element_forms(): images = jnp.dot(table, stacked, preferred_element_type=jnp.float32)  13.4 us
    ppermute x1, waiting for transfers between devices, padded_2(): lax.ppermute(lax.slice_in_dim(block, 0, width, axis=dim), axis, backward)  5.49 us
    ppermute x1, starting transfers between devices, padded_2(): lax.ppermute(lax.slice_in_dim(block, block.shape[dim] - width, None, axis...  5.19 us
    psum x1, blocking collectives, local(): scaled = lax.psum(scaled.astype(jnp.bfloat16), 'mode').astype(jnp.float32)  3.49 us
    add x1, other arithmetic, local(): mass_total = mass_total + eigenvalues[index] * mass_form  2.71 us
  transfers between devices with their start and end apart: 3, of which 1 were waited for; matrix products, arithmetic and copies ran while one was open for 6% of the time, Pallas kernels for 0%

commit v1 on v0

v1 whole, which is shorter than its diff:
```python
import functools

import jax
import jax.numpy as jnp
import ml_dtypes
import numpy as np
from jax import lax
from jax.experimental import pallas as pl
from jax.experimental.pallas import tpu as pltpu
from jax.sharding import PartitionSpec as P

MESH = pl.DeviceIdType.MESH


def element_tables():
    poisson = 0.3
    lame_first = poisson / ((1.0 + poisson) * (1.0 - 2.0 * poisson))
    shear = 0.5 / (1.0 + poisson)
    elastic = np.zeros((6, 6))
    elastic[:3, :3] = lame_first
    for axis_bit in range(3):
        elastic[axis_bit, axis_bit] += 2.0 * shear
        elastic[axis_bit + 3, axis_bit + 3] = shear
    stiffness = np.zeros((24, 24))
    mass_small = np.zeros((8, 8))
    point = 1.0 / np.sqrt(3.0)
    for gauss in range(8):
        coords = [point * (2 * (gauss >> axis_bit & 1) - 1) for axis_bit in range(3)]
        shape_values = np.zeros(8)
        grads = np.zeros((3, 8))
        for corner in range(8):
            signs = [2 * (corner >> axis_bit & 1) - 1 for axis_bit in range(3)]
            factors = [1.0 + signs[axis_bit] * coords[axis_bit] for axis_bit in range(3)]
            shape_values[corner] = 0.125 * factors[0] * factors[1] * factors[2]
            grads[0, corner] = 0.25 * signs[0] * factors[1] * factors[2]
            grads[1, corner] = 0.25 * signs[1] * factors[0] * factors[2]
            grads[2, corner] = 0.25 * signs[2] * factors[0] * factors[1]
        strain = np.zeros((6, 24))
        for corner in range(8):
            column = 3 * corner
            strain[0, column] = grads[0, corner]
            strain[1, column + 1] = grads[1, corner]
            strain[2, column + 2] = grads[2, corner]
            strain[3, column] = grads[1, corner]
            strain[3, column + 1] = grads[0, corner]
            strain[4, column + 1] = grads[2, corner]
            strain[4, column + 2] = grads[1, corner]
            strain[5, column] = grads[2, corner]
            strain[5, column + 2] = grads[0, corner]
        stiffness = stiffness + strain.T @ elastic @ strain * 0.125
        mass_small = mass_small + np.outer(shape_values, shape_values) * 0.125
    mass = np.kron(mass_small, np.eye(3))
    return np.concatenate([stiffness, mass], 0).astype(np.float32)


def transformed_terms():
    table = element_tables().astype(ml_dtypes.bfloat16).astype(np.float64)
    change = np.ones((8, 8))
    for corner in range(8):
        for pattern in range(8):
            for bit in range(3):
                if pattern >> bit & 1 and not corner >> bit & 1:
                    change[corner, pattern] *= -1.0
    stiff, mass = (
        np.einsum("is,icjd,jt->sctd", change, part.reshape(8, 3, 8, 3), change).reshape(24, 24) / 64.0
        for part in (table[:24], table[24:])
    )
    assert np.abs(mass - np.diag(np.diag(mass))).max() < 1e-12
    squares, crosses = {}, {}
    for row in range(24):
        key = (round(stiff[row, row], 12), round(mass[row, row], 12))
        squares.setdefault(key, []).append(row)
        for column in range(row):
            value = round(stiff[row, column] + stiff[column, row], 12)
            if value != 0.0:
                crosses.setdefault(value, []).append((row, column))
    return squares, crosses


def next_in(value, axis):
    size = value.shape[axis]
    place = lax.broadcasted_iota(jnp.int32, value.shape, axis)
    return jnp.where(place == size - 1, 0.0, pltpu.roll(value, size - 1, axis))


def both_sides(value, steps, axis):
    size = value.shape[axis]
    place = lax.broadcasted_iota(jnp.int32, value.shape, axis)
    ahead = jnp.where(place >= size - steps, 0.0, pltpu.roll(value, size - steps, axis))
    behind = jnp.where(place < steps, 0.0, pltpu.roll(value, steps, axis))
    return ahead + behind


def plane_terms(plane):
    value = plane.astype(jnp.float32)
    ahead = next_in(value, 1)
    along_x = (value + ahead, ahead - value)
    shifted = [next_in(part, 0) for part in along_x]
    return [along_x[0] + shifted[0], along_x[1] + shifted[1], shifted[0] - along_x[0], shifted[1] - along_x[1]]


def add_all(values):
    values = list(values)
    while len(values) > 1:
        values = [sum(values[i : i + 2][1:], values[i]) for i in range(0, len(values), 2)]
    return values[0]


def element_form(low, high):
    squares, crosses = transformed_terms()
    wave = {}
    for component in range(3):
        for pattern in range(4):
            wave[3 * pattern + component] = low[component][pattern] + high[component][pattern]
            wave[3 * (pattern + 4) + component] = high[component][pattern] - low[component][pattern]
    stiff, by_mass = [], {}
    for (stiff_value, mass_value), rows in squares.items():
        total = add_all(wave[row] * wave[row] for row in rows)
        if stiff_value != 0.0:
            stiff.append(stiff_value * total)
        by_mass.setdefault(mass_value, []).append(total)
    for value, pairs in crosses.items():
        stiff.append(value * add_all(wave[row] * wave[column] for row, column in pairs))
    mass = [value * add_all(totals) for value, totals in by_mass.items()]
    return add_all(stiff), add_all(mass)


def filtered(near, one, two):
    def weight(square):
        return max(0.0, 2.5 - float(np.sqrt(square)))

    rings = {
        0: near,
        1: both_sides(near, 1, 0) + one,
        2: both_sides(one, 1, 0),
        4: both_sides(near, 2, 0) + two,
        5: both_sides(one, 2, 0) + both_sides(two, 1, 0),
    }

    def column(steps):
        return add_all(
            weight(square + steps * steps) * ring
            for square, ring in rings.items()
            if weight(square + steps * steps) > 0.0
        )

    return column(0) + both_sides(column(1), 1, 1) + both_sides(column(2), 2, 1)


def kernel(
    layers, groups, modes_ref, eigen_ref, density_ref, out_ref,
    field, upper, terms, dens, share,
    field_sem, dens_sem, plane_send, plane_recv, share_send, share_recv,
):
    grid, mode = lax.axis_index("grid"), lax.axis_index("mode")
    count, depth = modes_ref.shape[0], modes_ref.shape[2]
    height, width = modes_ref.shape[3:]
    last = layers - 1

    def load(index):
        return pltpu.make_async_copy(modes_ref.at[index], field.at[index], field_sem.at[index])

    for index in range(count):
        load(index).start()
    density_copy = pltpu.make_async_copy(density_ref, dens, dens_sem)
    density_copy.start()

    partners = [(step, turn) for step in (-1, 1, 0) for turn in range(groups) if (step, turn) != (0, 0)]

    def target(step, turn):
        return (grid + step, lax.rem(mode + turn, groups))

    def there(step, body):
        if step < 0:
            pl.when(grid > 0)(body)
        elif step > 0:
            pl.when(grid < last)(body)
        else:
            body()

    barrier = pltpu.get_barrier_semaphore()
    for step, turn in partners:
        there(step, lambda: pl.semaphore_signal(barrier, inc=1, device_id=target(step, turn), device_id_type=MESH))
    sides = jnp.minimum(grid, 1) + jnp.minimum(last - grid, 1)
    pl.semaphore_wait(barrier, groups - 1 + groups * sides)

    def plane_copy(index):
        return pltpu.make_async_remote_copy(
            src_ref=modes_ref.at[index, :, 0],
            dst_ref=upper.at[index],
            send_sem=plane_send.at[index],
            recv_sem=plane_recv.at[index],
            device_id=(jnp.maximum(grid - 1, 0), mode),
            device_id_type=MESH,
        )

    @pl.when(grid > 0)
    def _():
        for index in range(count):
            plane_copy(index).start()

    @pl.when(grid == last)
    def _():
        upper[...] = jnp.zeros_like(upper)
        share[2] = jnp.zeros_like(share[2])

    @pl.when(grid == 0)
    def _():
        share[0] = jnp.zeros_like(share[0])

    ones = jnp.ones((height, width), jnp.float32)
    totals = []
    for layer in range(depth):
        place = grid * depth + layer

        def inside(steps):
            low = jnp.minimum(jnp.maximum(place - steps + 1, 0), 1)
            high = jnp.minimum(jnp.maximum(layers * depth - place - steps, 0), 1)
            return (low + high).astype(jnp.float32) * ones

        totals.append(filtered(ones, inside(1), inside(2)))

    zeros = jnp.zeros((height, width), jnp.float32)

    def first(index, carry):
        load(index).wait()
        low = [plane_terms(field[index, component, 0]) for component in range(3)]
        high = [plane_terms(field[index, component, 1]) for component in range(3)]
        for component in range(3):
            for pattern in range(4):
                terms[index, component, pattern] = high[component][pattern]
        stiff, mass = element_form(low, high)
        return carry[0] + stiff, carry[1] + eigen_ref[index] * mass

    def second(index, carry):
        @pl.when(grid < last)
        def _():
            plane_copy(index).wait_recv()

        low = [[terms[index, component, pattern] for pattern in range(4)] for component in range(3)]
        high = [plane_terms(upper[index, component]) for component in range(3)]
        stiff, mass = element_form(low, high)
        return carry[0] + stiff, carry[1] + eigen_ref[index] * mass

    def share_copy(layer, step, turn):
        return pltpu.make_async_remote_copy(
            src_ref=share.at[1, mode, layer],
            dst_ref=share.at[1 - step, mode, layer],
            send_sem=share_send.at[layer, step + 1, turn],
            recv_sem=share_recv.at[layer, 1 - step, mode],
            device_id=target(step, turn),
            device_id_type=MESH,
        )

    def arrived(layer, step, turn):
        source = lax.rem(mode + turn, groups)
        return pltpu.make_async_remote_copy(
            src_ref=share.at[1, mode, layer],
            dst_ref=share.at[1 + step, source, layer],
            send_sem=share_send.at[layer, step + 1, turn],
            recv_sem=share_recv.at[layer, 1 + step, source],
            device_id=target(step, turn),
            device_id_type=MESH,
        )

    def finish(layer, stiff, mass):
        slope = 3.0 * (1.0 - 0.001) * dens[layer] * dens[layer]
        share[1, mode, layer] = ((slope * stiff - mass) / totals[layer]).astype(jnp.bfloat16)
        for step, turn in partners:
            there(step, lambda: share_copy(layer, step, turn).start())

    stiff, mass = lax.fori_loop(0, count, first, (zeros, zeros))
    density_copy.wait()
    finish(0, stiff, mass)
    stiff, mass = lax.fori_loop(0, count, second, (zeros, zeros))
    finish(1, stiff, mass)

    for layer in range(depth):
        for step, turn in partners:
            there(step, lambda: arrived(layer, step, turn).wait_recv())

    def whole(place, layer):
        return add_all(share[place, group, layer].astype(jnp.float32) for group in range(groups))

    stack = [whole(place, layer) for place in range(3) for layer in range(depth)]
    for layer in range(depth):
        at = depth + layer
        out_ref[layer] = filtered(stack[at], stack[at - 1] + stack[at + 1], stack[at - 2] + stack[at + 2])

    for layer in range(depth):
        for step, turn in partners:
            there(step, lambda: share_copy(layer, step, turn).wait_send())

    @pl.when(grid > 0)
    def _():
        for index in range(count):
            plane_copy(index).wait_send()


def local(layers, groups, modes, eigenvalues, density):
    count, _, depth, height, width = modes.shape
    assert depth == 2
    return pl.pallas_call(
        functools.partial(kernel, layers, groups),
        out_shape=jax.ShapeDtypeStruct(density.shape, jnp.float32),
        in_specs=[
            pl.BlockSpec(memory_space=pl.ANY),
            pl.BlockSpec(memory_space=pltpu.SMEM),
            pl.BlockSpec(memory_space=pl.ANY),
        ],
        out_specs=pl.BlockSpec(memory_space=pltpu.VMEM),
        scratch_shapes=[
            pltpu.VMEM(modes.shape, jnp.bfloat16),
            pltpu.VMEM((count, 3, height, width), jnp.bfloat16),
            pltpu.VMEM((count, 3, 4, height, width), jnp.float32),
            pltpu.VMEM(density.shape, jnp.float32),
            pltpu.VMEM((3, groups, depth, height, width), jnp.bfloat16),
            pltpu.SemaphoreType.DMA((count,)),
            pltpu.SemaphoreType.DMA,
            pltpu.SemaphoreType.DMA((count,)),
            pltpu.SemaphoreType.DMA((count,)),
            pltpu.SemaphoreType.DMA((depth, 3, groups)),
            pltpu.SemaphoreType.DMA((depth, 3, groups)),
        ],
        compiler_params=pltpu.CompilerParams(
            collective_id=0, has_side_effects=True, vmem_limit_bytes=24 * 1024 * 1024
        ),
        name="sensitivities",
    )(modes, eigenvalues, density)


def solution(mesh):
    in_specs = (P("mode", None, "grid", None, None), P("mode"), P("grid", None, None))
    body = functools.partial(local, mesh.shape["grid"], mesh.shape["mode"])
    return jax.shard_map(body, mesh=mesh, in_specs=in_specs, out_specs=P("grid", None, None), check_vma=False)
```

time: 121 us -> 16.2 us (0.13)
  the two profiles are of different devices: /device:TPU:6 before, /device:TPU:17 now
where the time goes in v1:
time: 16.2 us; the launch traced here: 16 us
  Pallas kernels  13 us (80%)
  local copies, waits for them, and re-layouts  2.96 us (18%)
    pallas_call x1, Pallas kernels, local(): pl.pallas_call(functools.partial(kernel, layers, groups), out_shape=jax.S...  13 us
    unnamed x7, local copies, waits for them, and re-layouts  2.96 us

profile of v1, /device:TPU:17, one launch (start us, length us, event | category | flops | bytes accessed | tf_op | source)
XLA Modules:
  0.0 16.0 jit_solution(14799559663609837488)
XLA Ops:
  0.0 0.0 copy-start
  0.0 0.9 %copy-done = bf16[4,3,2,32,128]{4,3,2,1,0:T(8,128)(2,1)S(1)} copy-done((bf16[4,3,2,32,128]{4,3,2,1,0:T(8,128)(2,1)S(1)}, bf16[4,3,2,32,128]{4,3,2,1,0:T(8,128)(2,1)}, u32[]{:S(2)}) %copy-start) | copy-done | bytes 196632
  0.9 0.0 copy-start.1
  0.9 0.8 %copy-done.1 = f32[2,32,128]{2,1,0:T(8,128)S(1)} copy-done((f32[2,32,128]{2,1,0:T(8,128)S(1)}, f32[2,32,128]{2,1,0:T(8,128)}, u32[]{:S(2)}) %copy-start.1) | copy-done | bytes 32792
  1.7 0.0 copy-start.2
  1.7 0.7 %copy-done.2 = f32[4]{0:T(128)S(1)} copy-done((f32[4]{0:T(128)S(1)}, f32[4]{0:T(128)}, u32[]{:S(2)}) %copy-start.2) | copy-done | bytes 40
  2.3 13.0 %sensitivities.1 = f32[2,32,128]{2,1,0:T(8,128)S(1)} custom-call(bf16[4,3,2,32,128]{4,3,2,1,0:T(8,128)(2,1)S(1)} %copy-done, f32[4]{0:T(128)S(1)} %copy-done.2, f32[2,32,128]{2,1,0:T(8,128)S(1)} %copy-done.1), custom_call_target="tpu_custom_call" | custom-call | tf_op jit(solution)/shard_map/sensitivities/pallas_call | solution.py:303
  15.3 0.6 %copy.5 = f32[2,32,128]{2,1,0:T(8,128)} copy(f32[2,32,128]{2,1,0:T(8,128)S(1)} %sensitivities.1) | data formatting | bytes 65536
Async XLA Ops:
  0.0 0.9 %copy-start = (bf16[4,3,2,32,128]{4,3,2,1,0:T(8,128)(2,1)S(1)}, bf16[4,3,2,32,128]{4,3,2,1,0:T(8,128)(2,1)}, u32[]{:S(2)}) copy-start(bf16[4,3,2,32,128]{4,3,2,1,0:T(8,128)(2,1)} %modes_ref.1) | copy-start | bytes 589828
  0.9 0.8 %copy-start.1 = (f32[2,32,128]{2,1,0:T(8,128)S(1)}, f32[2,32,128]{2,1,0:T(8,128)}, u32[]{:S(2)}) copy-start(f32[2,32,128]{2,1,0:T(8,128)} %density_ref.1) | copy-start | bytes 98308
  1.7 0.7 %copy-start.2 = (f32[4]{0:T(128)S(1)}, f32[4]{0:T(128)}, u32[]{:S(2)}) copy-start(f32[4]{0:T(128)} %eigen_ref.1) | copy-start | bytes 52

commit v2 on v1

--- a/solution.py
+++ b/solution.py
@@ -148,22 +148,14 @@
 
 
 def kernel(
-    layers, groups, modes_ref, eigen_ref, density_ref, out_ref,
-    field, upper, terms, dens, share,
-    field_sem, dens_sem, plane_send, plane_recv, share_send, share_recv,
+    layers, groups, modes_ref, eigenvalues_ref, density_ref, out_ref,
+    eigen_ref, field, upper, terms, dens, share,
+    eigen_sem, field_sem, dens_sem, plane_send, plane_recv, share_send, share_recv,
 ):
     grid, mode = lax.axis_index("grid"), lax.axis_index("mode")
     count, depth = modes_ref.shape[0], modes_ref.shape[2]
     height, width = modes_ref.shape[3:]
     last = layers - 1
-
-    def load(index):
-        return pltpu.make_async_copy(modes_ref.at[index], field.at[index], field_sem.at[index])
-
-    for index in range(count):
-        load(index).start()
-    density_copy = pltpu.make_async_copy(density_ref, dens, dens_sem)
-    density_copy.start()
 
     partners = [(step, turn) for step in (-1, 1, 0) for turn in range(groups) if (step, turn) != (0, 0)]
 
@@ -181,6 +173,17 @@
     barrier = pltpu.get_barrier_semaphore()
     for step, turn in partners:
         there(step, lambda: pl.semaphore_signal(barrier, inc=1, device_id=target(step, turn), device_id_type=MESH))
+
+    def load(index):
+        return pltpu.make_async_copy(modes_ref.at[index], field.at[index], field_sem.at[index])
+
+    eigen_copy = pltpu.make_async_copy(eigenvalues_ref, eigen_ref, eigen_sem)
+    eigen_copy.start()
+    for index in range(count):
+        load(index).start()
+    density_copy = pltpu.make_async_copy(density_ref, dens, dens_sem)
+    density_copy.start()
+
     sides = jnp.minimum(grid, 1) + jnp.minimum(last - grid, 1)
     pl.semaphore_wait(barrier, groups - 1 + groups * sides)
 
@@ -269,6 +272,7 @@
         for step, turn in partners:
             there(step, lambda: share_copy(layer, step, turn).start())
 
+    eigen_copy.wait()
     stiff, mass = lax.fori_loop(0, count, first, (zeros, zeros))
     density_copy.wait()
     finish(0, stiff, mass)
@@ -304,17 +308,19 @@
         functools.partial(kernel, layers, groups),
         out_shape=jax.ShapeDtypeStruct(density.shape, jnp.float32),
         in_specs=[
-            pl.BlockSpec(memory_space=pl.ANY),
-            pl.BlockSpec(memory_space=pltpu.SMEM),
-            pl.BlockSpec(memory_space=pl.ANY),
+            pl.BlockSpec(memory_space=pltpu.HBM),
+            pl.BlockSpec(memory_space=pltpu.HBM),
+            pl.BlockSpec(memory_space=pltpu.HBM),
         ],
         out_specs=pl.BlockSpec(memory_space=pltpu.VMEM),
         scratch_shapes=[
+            pltpu.SMEM(eigenvalues.shape, jnp.float32),
             pltpu.VMEM(modes.shape, jnp.bfloat16),
             pltpu.VMEM((count, 3, height, width), jnp.bfloat16),
             pltpu.VMEM((count, 3, 4, height, width), jnp.float32),
             pltpu.VMEM(density.shape, jnp.float32),
             pltpu.VMEM((3, groups, depth, height, width), jnp.bfloat16),
+            pltpu.SemaphoreType.DMA,
             pltpu.SemaphoreType.DMA((count,)),
             pltpu.SemaphoreType.DMA,
             pltpu.SemaphoreType.DMA((count,)),

time: 16.2 us -> 15.3 us (0.944)
  Pallas kernels: 13 us -> 12.1 us
    pallas_call x1, Pallas kernels: 13 us -> 12.1 us  [local(): pl.pallas_call(functools.partial(kernel, layers, groups), out_shape=jax.S...]
where the time goes in v2:
time: 15.3 us; the launch traced here: 15.1 us
  Pallas kernels  12.1 us (79%)
  local copies, waits for them, and re-layouts  2.96 us (19%)
    pallas_call x1, Pallas kernels, local(): pl.pallas_call(functools.partial(kernel, layers, groups), out_shape=jax.S...  12.1 us
    unnamed x7, local copies, waits for them, and re-layouts  2.96 us

profile of v2, /device:TPU:17, one launch (start us, length us, event | category | flops | bytes accessed | tf_op | source)
XLA Modules:
  0.0 15.1 jit_solution(3391360219705377345)
XLA Ops:
  0.0 0.0 copy-start
  0.0 0.9 %copy-done = bf16[4,3,2,32,128]{4,3,2,1,0:T(8,128)(2,1)S(1)} copy-done((bf16[4,3,2,32,128]{4,3,2,1,0:T(8,128)(2,1)S(1)}, bf16[4,3,2,32,128]{4,3,2,1,0:T(8,128)(2,1)}, u32[]{:S(2)}) %copy-start) | copy-done | bytes 196632
  0.9 0.0 copy-start.1
  0.9 0.8 %copy-done.1 = f32[2,32,128]{2,1,0:T(8,128)S(1)} copy-done((f32[2,32,128]{2,1,0:T(8,128)S(1)}, f32[2,32,128]{2,1,0:T(8,128)}, u32[]{:S(2)}) %copy-start.1) | copy-done | bytes 32792
  1.7 0.0 copy-start.2
  1.7 0.7 %copy-done.2 = f32[4]{0:T(128)S(1)} copy-done((f32[4]{0:T(128)S(1)}, f32[4]{0:T(128)}, u32[]{:S(2)}) %copy-start.2) | copy-done | bytes 40
  2.3 12.1 %sensitivities.1 = f32[2,32,128]{2,1,0:T(8,128)S(1)} custom-call(bf16[4,3,2,32,128]{4,3,2,1,0:T(8,128)(2,1)S(1)} %copy-done, f32[4]{0:T(128)S(1)} %copy-done.2, f32[2,32,128]{2,1,0:T(8,128)S(1)} %copy-done.1), custom_call_target="tpu_custom_call" | custom-call | tf_op jit(solution)/shard_map/sensitivities/pallas_call | solution.py:307
  14.5 0.6 %copy.5 = f32[2,32,128]{2,1,0:T(8,128)} copy(f32[2,32,128]{2,1,0:T(8,128)S(1)} %sensitivities.1) | data formatting | bytes 65536
Async XLA Ops:
  0.0 0.9 %copy-start = (bf16[4,3,2,32,128]{4,3,2,1,0:T(8,128)(2,1)S(1)}, bf16[4,3,2,32,128]{4,3,2,1,0:T(8,128)(2,1)}, u32[]{:S(2)}) copy-start(bf16[4,3,2,32,128]{4,3,2,1,0:T(8,128)(2,1)} %modes_ref.1) | copy-start | bytes 589828
  0.9 0.8 %copy-start.1 = (f32[2,32,128]{2,1,0:T(8,128)S(1)}, f32[2,32,128]{2,1,0:T(8,128)}, u32[]{:S(2)}) copy-start(f32[2,32,128]{2,1,0:T(8,128)} %density_ref.1) | copy-start | bytes 98308
  1.7 0.7 %copy-start.2 = (f32[4]{0:T(128)S(1)}, f32[4]{0:T(128)}, u32[]{:S(2)}) copy-start(f32[4]{0:T(128)} %eigenvalues_ref.1) | copy-start | bytes 52

commit v3 on v2

--- a/solution.py
+++ b/solution.py
@@ -329,7 +329,7 @@
             pltpu.SemaphoreType.DMA((depth, 3, groups)),
         ],
         compiler_params=pltpu.CompilerParams(
-            collective_id=0, has_side_effects=True, vmem_limit_bytes=24 * 1024 * 1024
+            collective_id=0, has_side_effects=True, vmem_limit_bytes=60 * 1024 * 1024
         ),
         name="sensitivities",
     )(modes, eigenvalues, density)

time: 15.3 us -> 14.5 us (0.948)
  local copies, waits for them, and re-layouts: 2.96 us -> 1.38 us
  Pallas kernels: 12.1 us -> 12.9 us
    unnamed x7 -> x1, local copies, waits for them, and re-layouts: 2.96 us -> 1.38 us
    pallas_call x1, Pallas kernels: 12.1 us -> 12.9 us  [local(): pl.pallas_call(functools.partial(kernel, layers, groups), out_shape=jax.S...]
where the time goes in v3:
time: 14.5 us; the launch traced here: 14.3 us
  Pallas kernels  12.9 us (89%)
  local copies, waits for them, and re-layouts  1.38 us (10%)
    pallas_call x1, Pallas kernels, local(): pl.pallas_call(functools.partial(kernel, layers, groups), out_shape=jax.S...  12.9 us
    unnamed x1, local copies, waits for them, and re-layouts  1.38 us

profile of v3, /device:TPU:17, one launch (start us, length us, event | category | flops | bytes accessed | tf_op | source)
XLA Modules:
  0.0 14.3 jit_solution(9282095680409941324)
XLA Ops:
  0.0 12.9 %sensitivities.1 = f32[2,32,128]{2,1,0:T(8,128)} custom-call(bf16[4,3,2,32,128]{4,3,2,1,0:T(8,128)(2,1)} %modes_ref.1, f32[4]{0:T(128)} %eigenvalues_ref.1, f32[2,32,128]{2,1,0:T(8,128)} %density_ref.1), custom_call_target="tpu_custom_call" | custom-call | tf_op jit(solution)/shard_map/sensitivities/pallas_call | solution.py:307
  12.9 1.4 %copy.5 = f32[2,32,128]{2,1,0:T(8,128)} copy(f32[2,32,128]{2,1,0:T(8,128)} %sensitivities.1) | data formatting | bytes 65536

commit v4 on v3

--- a/solution.py
+++ b/solution.py
@@ -306,7 +306,7 @@
     assert depth == 2
     return pl.pallas_call(
         functools.partial(kernel, layers, groups),
-        out_shape=jax.ShapeDtypeStruct(density.shape, jnp.float32),
+        out_shape=pltpu.VMEM(density.shape, jnp.float32),
         in_specs=[
             pl.BlockSpec(memory_space=pltpu.HBM),
             pl.BlockSpec(memory_space=pltpu.HBM),

time: 14.5 us -> 13.1 us (0.903)
  local copies, waits for them, and re-layouts: 1.38 us -> 0.62 us
  Pallas kernels: 12.9 us -> 12.3 us
    unnamed x1, local copies, waits for them, and re-layouts: 1.38 us -> 0.62 us
    pallas_call x1, Pallas kernels: 12.9 us -> 12.3 us  [local(): pl.pallas_call(functools.partial(kernel, layers, groups), out_shape=pltpu...]
where the time goes in v4:
time: 13.1 us; the launch traced here: 13 us
  Pallas kernels  12.3 us (94%)
  local copies, waits for them, and re-layouts  0.62 us (5%)
    pallas_call x1, Pallas kernels, local(): pl.pallas_call(functools.partial(kernel, layers, groups), out_shape=pltpu...  12.3 us
    unnamed x1, local copies, waits for them, and re-layouts  0.62 us

profile of v4, /device:TPU:17, one launch (start us, length us, event | category | flops | bytes accessed | tf_op | source)
XLA Modules:
  0.0 13.0 jit_solution(1254166486396455443)
XLA Ops:
  0.0 12.3 %sensitivities.1 = f32[2,32,128]{2,1,0:T(8,128)S(1)} custom-call(bf16[4,3,2,32,128]{4,3,2,1,0:T(8,128)(2,1)} %modes_ref.1, f32[4]{0:T(128)} %eigenvalues_ref.1, f32[2,32,128]{2,1,0:T(8,128)} %density_ref.1), custom_call_target="tpu_custom_call" | custom-call | tf_op jit(solution)/shard_map/sensitivities/pallas_call | solution.py:307
  12.3 0.6 %copy.5 = f32[2,32,128]{2,1,0:T(8,128)} copy(f32[2,32,128]{2,1,0:T(8,128)S(1)} %sensitivities.1) | data formatting | bytes 65536

commit v5 on v4

--- a/solution.py
+++ b/solution.py
@@ -125,26 +125,33 @@
     return add_all(stiff), add_all(mass)
 
 
-def filtered(near, one, two):
+def ring_columns(near, one, two):
     def weight(square):
         return max(0.0, 2.5 - float(np.sqrt(square)))
 
-    rings = {
-        0: near,
-        1: both_sides(near, 1, 0) + one,
-        2: both_sides(one, 1, 0),
-        4: both_sides(near, 2, 0) + two,
-        5: both_sides(one, 2, 0) + both_sides(two, 1, 0),
-    }
-
-    def column(steps):
-        return add_all(
+    rings = []
+    for square, layer in ((0, near), (1, one), (4, two)):
+        if layer is not None:
+            rings.append((square, layer))
+            for steps in (1, 2):
+                if weight(square + steps * steps) > 0.0:
+                    rings.append((square + steps * steps, both_sides(layer, steps, 0)))
+    gathered = {}
+    for square, ring in rings:
+        gathered.setdefault(square, []).append(ring)
+    gathered = {square: add_all(parts) for square, parts in gathered.items()}
+    return [
+        add_all(
             weight(square + steps * steps) * ring
-            for square, ring in rings.items()
+            for square, ring in gathered.items()
             if weight(square + steps * steps) > 0.0
         )
-
-    return column(0) + both_sides(column(1), 1, 1) + both_sides(column(2), 2, 1)
+        for steps in range(3)
+    ]
+
+
+def along_rows(columns):
+    return columns[0] + both_sides(columns[1], 1, 1) + both_sides(columns[2], 2, 1)
 
 
 def kernel(
@@ -184,6 +191,27 @@
     density_copy = pltpu.make_async_copy(density_ref, dens, dens_sem)
     density_copy.start()
 
+    @pl.when(grid == last)
+    def _():
+        upper[...] = jnp.zeros_like(upper)
+        share[2] = jnp.zeros_like(share[2])
+
+    @pl.when(grid == 0)
+    def _():
+        share[0] = jnp.zeros_like(share[0])
+
+    ones = jnp.ones((height, width), jnp.float32)
+    totals = []
+    for layer in range(depth):
+        place = grid * depth + layer
+
+        def inside(steps):
+            low = jnp.minimum(jnp.maximum(place - steps + 1, 0), 1)
+            high = jnp.minimum(jnp.maximum(layers * depth - place - steps, 0), 1)
+            return (low + high).astype(jnp.float32) * ones
+
+        totals.append(along_rows(ring_columns(ones, inside(1), inside(2))))
+
     sides = jnp.minimum(grid, 1) + jnp.minimum(last - grid, 1)
     pl.semaphore_wait(barrier, groups - 1 + groups * sides)
 
@@ -201,27 +229,6 @@
     def _():
         for index in range(count):
             plane_copy(index).start()
-
-    @pl.when(grid == last)
-    def _():
-        upper[...] = jnp.zeros_like(upper)
-        share[2] = jnp.zeros_like(share[2])
-
-    @pl.when(grid == 0)
-    def _():
-        share[0] = jnp.zeros_like(share[0])
-
-    ones = jnp.ones((height, width), jnp.float32)
-    totals = []
-    for layer in range(depth):
-        place = grid * depth + layer
-
-        def inside(steps):
-            low = jnp.minimum(jnp.maximum(place - steps + 1, 0), 1)
-            high = jnp.minimum(jnp.maximum(layers * depth - place - steps, 0), 1)
-            return (low + high).astype(jnp.float32) * ones
-
-        totals.append(filtered(ones, inside(1), inside(2)))
 
     zeros = jnp.zeros((height, width), jnp.float32)
 
@@ -279,17 +286,20 @@
     stiff, mass = lax.fori_loop(0, count, second, (zeros, zeros))
     finish(1, stiff, mass)
 
-    for layer in range(depth):
-        for step, turn in partners:
-            there(step, lambda: arrived(layer, step, turn).wait_recv())
-
     def whole(place, layer):
         return add_all(share[place, group, layer].astype(jnp.float32) for group in range(groups))
 
-    stack = [whole(place, layer) for place in range(3) for layer in range(depth)]
+    def await_layer(layer):
+        for step, turn in reversed(partners):
+            there(step, lambda: arrived(layer, step, turn).wait_recv())
+        return [whole(place, layer) for place in range(3)]
+
+    below, centre, above = await_layer(0)
+    early = [ring_columns(centre, None, below + above), ring_columns(None, centre + above, None)]
+    below, centre, above = await_layer(1)
+    late = [ring_columns(None, below + centre, None), ring_columns(centre, None, below + above)]
     for layer in range(depth):
-        at = depth + layer
-        out_ref[layer] = filtered(stack[at], stack[at - 1] + stack[at + 1], stack[at - 2] + stack[at + 2])
+        out_ref[layer] = along_rows([one + two for one, two in zip(early[layer], late[layer])])
 
     for layer in range(depth):
         for step, turn in partners:

time: 13.1 us -> 13.1 us (level)
  no operation moved by 1% of the time
where the time goes in v5:
time: 13.1 us; the launch traced here: 12.9 us
  Pallas kernels  12.3 us (94%)
  local copies, waits for them, and re-layouts  0.62 us (5%)
    pallas_call x1, Pallas kernels, local(): pl.pallas_call(functools.partial(kernel, layers, groups), out_shape=pltpu...  12.3 us
    unnamed x1, local copies, waits for them, and re-layouts  0.62 us

profile of v5, /device:TPU:17, one launch (start us, length us, event | category | flops | bytes accessed | tf_op | source)
XLA Modules:
  0.0 12.9 jit_solution(3965008604814842047)
XLA Ops:
  0.0 12.3 %sensitivities.1 = f32[2,32,128]{2,1,0:T(8,128)S(1)} custom-call(bf16[4,3,2,32,128]{4,3,2,1,0:T(8,128)(2,1)} %modes_ref.1, f32[4]{0:T(128)} %eigenvalues_ref.1, f32[2,32,128]{2,1,0:T(8,128)} %density_ref.1), custom_call_target="tpu_custom_call" | custom-call | tf_op jit(solution)/shard_map/sensitivities/pallas_call | solution.py:317
  12.3 0.6 %copy.5 = f32[2,32,128]{2,1,0:T(8,128)} copy(f32[2,32,128]{2,1,0:T(8,128)S(1)} %sensitivities.1) | data formatting | bytes 65536

commit v6 on v5

--- a/solution.py
+++ b/solution.py
@@ -156,7 +156,7 @@
 
 def kernel(
     layers, groups, modes_ref, eigenvalues_ref, density_ref, out_ref,
-    eigen_ref, field, upper, terms, dens, share,
+    eigen_ref, field, upper, terms, dens, share, sums,
     eigen_sem, field_sem, dens_sem, plane_send, plane_recv, share_send, share_recv,
 ):
     grid, mode = lax.axis_index("grid"), lax.axis_index("mode")
@@ -164,16 +164,17 @@
     height, width = modes_ref.shape[3:]
     last = layers - 1
 
-    partners = [(step, turn) for step in (-1, 1, 0) for turn in range(groups) if (step, turn) != (0, 0)]
+    partners = [(step, turn) for step in (-2, 2, -1, 1, 0) for turn in range(groups) if (step, turn) != (0, 0)]
+    half = count // 2
 
     def target(step, turn):
         return (grid + step, lax.rem(mode + turn, groups))
 
     def there(step, body):
         if step < 0:
-            pl.when(grid > 0)(body)
+            pl.when(grid + step >= 0)(body)
         elif step > 0:
-            pl.when(grid < last)(body)
+            pl.when(grid + step <= last)(body)
         else:
             body()
 
@@ -188,21 +189,29 @@
     eigen_copy.start()
     for index in range(count):
         load(index).start()
-    density_copy = pltpu.make_async_copy(density_ref, dens, dens_sem)
+    density_copy = pltpu.make_async_copy(density_ref, dens.at[:depth], dens_sem)
     density_copy.start()
 
     @pl.when(grid == last)
     def _():
-        upper[...] = jnp.zeros_like(upper)
-        share[2] = jnp.zeros_like(share[2])
+        upper[:half] = jnp.zeros_like(upper[:half])
+        share[0, 2] = jnp.zeros_like(share[0, 2])
+        share[1, 2] = jnp.zeros_like(share[1, 2])
+        share[2, 1] = jnp.zeros_like(share[2, 1])
+
+    @pl.when(grid >= last - 1)
+    def _():
+        share[2, 2] = jnp.zeros_like(share[2, 2])
 
     @pl.when(grid == 0)
     def _():
-        share[0] = jnp.zeros_like(share[0])
+        share[0, 0] = jnp.zeros_like(share[0, 0])
+        share[1, 0] = jnp.zeros_like(share[1, 0])
+        share[2, 0] = jnp.zeros_like(share[2, 0])
 
     ones = jnp.ones((height, width), jnp.float32)
     totals = []
-    for layer in range(depth):
+    for layer in (0, 1, -1):
         place = grid * depth + layer
 
         def inside(steps):
@@ -212,23 +221,45 @@
 
         totals.append(along_rows(ring_columns(ones, inside(1), inside(2))))
 
-    sides = jnp.minimum(grid, 1) + jnp.minimum(last - grid, 1)
+    sides = jnp.minimum(grid, 2) + jnp.minimum(last - grid, 2)
     pl.semaphore_wait(barrier, groups - 1 + groups * sides)
 
     def plane_copy(index):
+        up = index >= half
+        return pltpu.make_async_remote_copy(
+            src_ref=modes_ref.at[index, :, depth - 1 if up else 0],
+            dst_ref=upper.at[index],
+            send_sem=plane_send.at[index],
+            recv_sem=plane_recv.at[index],
+            device_id=target(1 if up else -1, 0),
+            device_id_type=MESH,
+        )
+
+    def density_up():
+        return pltpu.make_async_remote_copy(
+            src_ref=density_ref.at[depth - 1],
+            dst_ref=dens.at[depth],
+            send_sem=plane_send.at[count],
+            recv_sem=plane_recv.at[count],
+            device_id=target(1, 0),
+            device_id_type=MESH,
+        )
+
+    def arriving(index):
         return pltpu.make_async_remote_copy(
             src_ref=modes_ref.at[index, :, 0],
             dst_ref=upper.at[index],
             send_sem=plane_send.at[index],
             recv_sem=plane_recv.at[index],
-            device_id=(jnp.maximum(grid - 1, 0), mode),
+            device_id=target(0, 0),
             device_id_type=MESH,
         )
 
-    @pl.when(grid > 0)
-    def _():
-        for index in range(count):
-            plane_copy(index).start()
+    down, up = range(half), range(half, count)
+    for one, two in zip(down, up):
+        there(-1, lambda: plane_copy(one).start())
+        there(1, lambda: plane_copy(two).start())
+    there(1, lambda: density_up().start())
 
     zeros = jnp.zeros((height, width), jnp.float32)
 
@@ -236,84 +267,126 @@
         load(index).wait()
         low = [plane_terms(field[index, component, 0]) for component in range(3)]
         high = [plane_terms(field[index, component, 1]) for component in range(3)]
+        kept = jnp.where(index < half, 1.0, 0.0)
         for component in range(3):
             for pattern in range(4):
-                terms[index, component, pattern] = high[component][pattern]
+                top, bottom = high[component][pattern], low[component][pattern]
+                terms[index, component, pattern] = kept * top + (1.0 - kept) * bottom
         stiff, mass = element_form(low, high)
         return carry[0] + stiff, carry[1] + eigen_ref[index] * mass
 
-    def second(index, carry):
-        @pl.when(grid < last)
-        def _():
-            plane_copy(index).wait_recv()
-
-        low = [[terms[index, component, pattern] for pattern in range(4)] for component in range(3)]
-        high = [plane_terms(upper[index, component]) for component in range(3)]
+    def kept_terms(index):
+        return [[terms[index, component, pattern] for pattern in range(4)] for component in range(3)]
+
+    def add_form(layer, index, low, high):
         stiff, mass = element_form(low, high)
-        return carry[0] + stiff, carry[1] + eigen_ref[index] * mass
-
-    def share_copy(layer, step, turn):
+        sums[layer, 0] += stiff
+        sums[layer, 1] += eigen_ref[index] * mass
+
+    reach = {0: (-1, 1, 0), 1: (-1, 1, 0), 2: (-2, -1, 0)}
+
+    def sends(kind):
+        return [(step, turn) for step in reach[kind] for turn in range(groups) if (step, turn) != (0, 0)]
+
+    def slot(kind, source):
+        return source if kind == 2 else source + 1
+
+    def share_copy(kind, step, turn):
         return pltpu.make_async_remote_copy(
-            src_ref=share.at[1, mode, layer],
-            dst_ref=share.at[1 - step, mode, layer],
-            send_sem=share_send.at[layer, step + 1, turn],
-            recv_sem=share_recv.at[layer, 1 - step, mode],
+            src_ref=share.at[kind, slot(kind, 0), mode],
+            dst_ref=share.at[kind, slot(kind, -step), mode],
+            send_sem=share_send.at[kind, slot(kind, -step), turn],
+            recv_sem=share_recv.at[kind, slot(kind, -step), mode],
             device_id=target(step, turn),
             device_id_type=MESH,
         )
 
-    def arrived(layer, step, turn):
-        source = lax.rem(mode + turn, groups)
+    def arrived(kind, source, turn):
+        group = lax.rem(mode + turn, groups)
         return pltpu.make_async_remote_copy(
-            src_ref=share.at[1, mode, layer],
-            dst_ref=share.at[1 + step, source, layer],
-            send_sem=share_send.at[layer, step + 1, turn],
-            recv_sem=share_recv.at[layer, 1 + step, source],
-            device_id=target(step, turn),
+            src_ref=share.at[kind, slot(kind, 0), mode],
+            dst_ref=share.at[kind, slot(kind, source), group],
+            send_sem=share_send.at[kind, slot(kind, source), turn],
+            recv_sem=share_recv.at[kind, slot(kind, source), group],
+            device_id=target(0, 0),
             device_id_type=MESH,
         )
 
-    def finish(layer, stiff, mass):
-        slope = 3.0 * (1.0 - 0.001) * dens[layer] * dens[layer]
-        share[1, mode, layer] = ((slope * stiff - mass) / totals[layer]).astype(jnp.bfloat16)
-        for step, turn in partners:
-            there(step, lambda: share_copy(layer, step, turn).start())
+    def finish(kind, density, stiff, mass):
+        slope = 3.0 * (1.0 - 0.001) * density * density
+        share[kind, slot(kind, 0), mode] = ((slope * stiff - mass) / totals[kind]).astype(jnp.bfloat16)
+        for step, turn in sends(kind):
+            there(step, lambda: share_copy(kind, step, turn).start())
 
     eigen_copy.wait()
     stiff, mass = lax.fori_loop(0, count, first, (zeros, zeros))
     density_copy.wait()
-    finish(0, stiff, mass)
-    stiff, mass = lax.fori_loop(0, count, second, (zeros, zeros))
-    finish(1, stiff, mass)
-
-    def whole(place, layer):
-        return add_all(share[place, group, layer].astype(jnp.float32) for group in range(groups))
-
-    def await_layer(layer):
-        for step, turn in reversed(partners):
-            there(step, lambda: arrived(layer, step, turn).wait_recv())
-        return [whole(place, layer) for place in range(3)]
-
-    below, centre, above = await_layer(0)
+    finish(0, dens[0], stiff, mass)
+    sums[...] = jnp.zeros_like(sums)
+
+    @pl.when(grid == last)
+    def _():
+        @pl.loop(half, count)
+        def _(index):
+            low = [plane_terms(field[index, component, 1]) for component in range(3)]
+            add_form(0, index, low, [[zeros] * 4] * 3)
+
+    @pl.loop(0, half)
+    def _(index):
+        @pl.when(grid < last)
+        def _():
+            arriving(index).wait_recv()
+
+        add_form(0, index, kept_terms(index), [plane_terms(upper[index, component]) for component in range(3)])
+
+    finish(1, dens[1], sums[0, 0], sums[0, 1])
+
+    @pl.when(grid > 0)
+    def _():
+        @pl.loop(half, count)
+        def _(index):
+            arriving(index).wait_recv()
+            add_form(1, index, [plane_terms(upper[index, component]) for component in range(3)], kept_terms(index))
+
+        density_up().wait_recv()
+        finish(2, dens[depth], sums[1, 0], sums[1, 1])
+
+    def whole(kind, place):
+        return add_all(share[kind, place, group].astype(jnp.float32) for group in range(groups))
+
+    def await_kind(kind):
+        for step, turn in reversed(sends(kind)):
+            pair = functools.partial(there, -step)
+            body = lambda: arrived(kind, -step, turn).wait_recv()
+            if kind == 2 and step == 0:
+                pl.when(grid > 0)(body)
+            else:
+                pair(body)
+        return [whole(kind, place) for place in range(3)]
+
+    below, centre, above = await_kind(0)
     early = [ring_columns(centre, None, below + above), ring_columns(None, centre + above, None)]
-    below, centre, above = await_layer(1)
+    below, centre, above = [one + two for one, two in zip(await_kind(1), await_kind(2))]
     late = [ring_columns(None, below + centre, None), ring_columns(centre, None, below + above)]
     for layer in range(depth):
         out_ref[layer] = along_rows([one + two for one, two in zip(early[layer], late[layer])])
 
-    for layer in range(depth):
-        for step, turn in partners:
-            there(step, lambda: share_copy(layer, step, turn).wait_send())
-
-    @pl.when(grid > 0)
-    def _():
-        for index in range(count):
-            plane_copy(index).wait_send()
+    for kind in range(3):
+        for step, turn in sends(kind):
+            body = lambda: share_copy(kind, step, turn).wait_send()
+            if kind == 2 and step == 0:
+                pl.when(grid > 0)(body)
+            else:
+                there(step, body)
+    for one, two in zip(down, up):
+        there(-1, lambda: plane_copy(one).wait_send())
+        there(1, lambda: plane_copy(two).wait_send())
+    there(1, lambda: density_up().wait_send())
 
 
 def local(layers, groups, modes, eigenvalues, density):
     count, _, depth, height, width = modes.shape
-    assert depth == 2
+    assert depth == 2 and count % 2 == 0
     return pl.pallas_call(
         functools.partial(kernel, layers, groups),
         out_shape=pltpu.VMEM(density.shape, jnp.float32),
@@ -328,15 +401,16 @@
             pltpu.VMEM(modes.shape, jnp.bfloat16),
             pltpu.VMEM((count, 3, height, width), jnp.bfloat16),
             pltpu.VMEM((count, 3, 4, height, width), jnp.float32),
-            pltpu.VMEM(density.shape, jnp.float32),
-            pltpu.VMEM((3, groups, depth, height, width), jnp.bfloat16),
+            pltpu.VMEM((depth + 1, height, width), jnp.float32),
+            pltpu.VMEM((3, 3, groups, height, width), jnp.bfloat16),
+            pltpu.VMEM((2, 2, height, width), jnp.float32),
             pltpu.SemaphoreType.DMA,
             pltpu.SemaphoreType.DMA((count,)),
             pltpu.SemaphoreType.DMA,
-            pltpu.SemaphoreType.DMA((count,)),
-            pltpu.SemaphoreType.DMA((count,)),
-            pltpu.SemaphoreType.DMA((depth, 3, groups)),
-            pltpu.SemaphoreType.DMA((depth, 3, groups)),
+            pltpu.SemaphoreType.DMA((count + 1,)),
+            pltpu.SemaphoreType.DMA((count + 1,)),
+            pltpu.SemaphoreType.DMA((3, 3, groups)),
+            pltpu.SemaphoreType.DMA((3, 3, groups)),
         ],
         compiler_params=pltpu.CompilerParams(
             collective_id=0, has_side_effects=True, vmem_limit_bytes=60 * 1024 * 1024

time: 13.1 us -> 12.9 us (0.985)
  the two profiles are of different devices: /device:TPU:17 before, /device:TPU:0 now
where the time goes in v6:
time: 12.9 us; the launch traced here: 12.8 us
  Pallas kernels  12.2 us (95%)
  local copies, waits for them, and re-layouts  0.62 us (5%)
    pallas_call x1, Pallas kernels, local(): pl.pallas_call(functools.partial(kernel, layers, groups), out_shape=pltpu...  12.2 us
    unnamed x1, local copies, waits for them, and re-layouts  0.62 us

profile of v6, /device:TPU:0, one launch (start us, length us, event | category | flops | bytes accessed | tf_op | source)
XLA Modules:
  0.0 12.8 jit_solution(12848907985054268670)
XLA Ops:
  0.0 12.2 %sensitivities.1 = f32[2,32,128]{2,1,0:T(8,128)S(1)} custom-call(bf16[4,3,2,32,128]{4,3,2,1,0:T(8,128)(2,1)} %modes_ref.1, f32[4]{0:T(128)} %eigenvalues_ref.1, f32[2,32,128]{2,1,0:T(8,128)} %density_ref.1), custom_call_target="tpu_custom_call" | custom-call | tf_op jit(solution)/shard_map/sensitivities/pallas_call | solution.py:390
  12.2 0.6 %copy.5 = f32[2,32,128]{2,1,0:T(8,128)} copy(f32[2,32,128]{2,1,0:T(8,128)S(1)} %sensitivities.1) | data formatting | bytes 65536

commit v7 on v6

--- a/solution.py
+++ b/solution.py
@@ -264,7 +264,6 @@
     zeros = jnp.zeros((height, width), jnp.float32)
 
     def first(index, carry):
-        load(index).wait()
         low = [plane_terms(field[index, component, 0]) for component in range(3)]
         high = [plane_terms(field[index, component, 1]) for component in range(3)]
         kept = jnp.where(index < half, 1.0, 0.0)
@@ -319,7 +318,9 @@
             there(step, lambda: share_copy(kind, step, turn).start())
 
     eigen_copy.wait()
-    stiff, mass = lax.fori_loop(0, count, first, (zeros, zeros))
+    for index in range(count):
+        load(index).wait()
+    stiff, mass = lax.fori_loop(0, count, first, (zeros, zeros), unroll=2)
     density_copy.wait()
     finish(0, dens[0], stiff, mass)
     sums[...] = jnp.zeros_like(sums)

time: 12.9 us -> 12.9 us (level)
  no operation moved by 1% of the time
where the time goes in v7:
time: 12.9 us; the launch traced here: 12.8 us
  Pallas kernels  12.2 us (95%)
  local copies, waits for them, and re-layouts  0.62 us (5%)
    pallas_call x1, Pallas kernels, local(): pl.pallas_call(functools.partial(kernel, layers, groups), out_shape=pltpu...  12.2 us
    unnamed x1, local copies, waits for them, and re-layouts  0.62 us

profile of v7, /device:TPU:0, one launch (start us, length us, event | category | flops | bytes accessed | tf_op | source)
XLA Modules:
  0.0 12.8 jit_solution(8203756356709158058)
XLA Ops:
  0.0 12.2 %sensitivities.1 = f32[2,32,128]{2,1,0:T(8,128)S(1)} custom-call(bf16[4,3,2,32,128]{4,3,2,1,0:T(8,128)(2,1)} %modes_ref.1, f32[4]{0:T(128)} %eigenvalues_ref.1, f32[2,32,128]{2,1,0:T(8,128)} %density_ref.1), custom_call_target="tpu_custom_call" | custom-call | tf_op jit(solution)/shard_map/sensitivities/pallas_call | solution.py:391
  12.2 0.6 %copy.5 = f32[2,32,128]{2,1,0:T(8,128)} copy(f32[2,32,128]{2,1,0:T(8,128)S(1)} %sensitivities.1) | data formatting | bytes 65536

commit v8 on v7

--- a/solution.py
+++ b/solution.py
@@ -325,6 +325,16 @@
     finish(0, dens[0], stiff, mass)
     sums[...] = jnp.zeros_like(sums)
 
+    @pl.when(grid > 0)
+    def _():
+        @pl.loop(half, count)
+        def _(index):
+            arriving(index).wait_recv()
+            add_form(1, index, [plane_terms(upper[index, component]) for component in range(3)], kept_terms(index))
+
+        density_up().wait_recv()
+        finish(2, dens[depth], sums[1, 0], sums[1, 1])
+
     @pl.when(grid == last)
     def _():
         @pl.loop(half, count)
@@ -341,16 +351,6 @@
         add_form(0, index, kept_terms(index), [plane_terms(upper[index, component]) for component in range(3)])
 
     finish(1, dens[1], sums[0, 0], sums[0, 1])
-
-    @pl.when(grid > 0)
-    def _():
-        @pl.loop(half, count)
-        def _(index):
-            arriving(index).wait_recv()
-            add_form(1, index, [plane_terms(upper[index, component]) for component in range(3)], kept_terms(index))
-
-        density_up().wait_recv()
-        finish(2, dens[depth], sums[1, 0], sums[1, 1])
 
     def whole(kind, place):
         return add_all(share[kind, place, group].astype(jnp.float32) for group in range(groups))

time: 12.9 us -> 13.1 us (1.016)
  no operation moved by 1% of the time
where the time goes in v8:
time: 13.1 us; the launch traced here: 12.9 us
  Pallas kernels  12.3 us (94%)
  local copies, waits for them, and re-layouts  0.62 us (5%)
    pallas_call x1, Pallas kernels, local(): pl.pallas_call(functools.partial(kernel, layers, groups), out_shape=pltpu...  12.3 us
    unnamed x1, local copies, waits for them, and re-layouts  0.62 us

profile of v8, /device:TPU:0, one launch (start us, length us, event | category | flops | bytes accessed | tf_op | source)
XLA Modules:
  0.0 12.9 jit_solution(14242791779264725374)
XLA Ops:
  0.0 12.3 %sensitivities.1 = f32[2,32,128]{2,1,0:T(8,128)S(1)} custom-call(bf16[4,3,2,32,128]{4,3,2,1,0:T(8,128)(2,1)} %modes_ref.1, f32[4]{0:T(128)} %eigenvalues_ref.1, f32[2,32,128]{2,1,0:T(8,128)} %density_ref.1), custom_call_target="tpu_custom_call" | custom-call | tf_op jit(solution)/shard_map/sensitivities/pallas_call | solution.py:391
  12.3 0.6 %copy.5 = f32[2,32,128]{2,1,0:T(8,128)} copy(f32[2,32,128]{2,1,0:T(8,128)S(1)} %sensitivities.1) | data formatting | bytes 65536
